TPU v7x, 32 devices: a whole 2x2x4 slice. The times are simulated.
32 devices in a mesh: gz: 2 (over y), spec: 16 (over z, x, core).
Axes of the slice: x: 2, y: 2, z: 4, core: 2. Of those that a mesh axis runs over, the one named last changes fastest.
Arguments:
- flux: bfloat16 [4096, 7168], P('spec', 'gz'), may hold values from -6 to 6
- ivar: bfloat16 [4096, 7168], P('spec', 'gz'), may hold values from 0.25 to 4
- mask: int32 [4096, 7168], P('spec', 'gz'), may hold values 0 or 1
- table: bfloat16 [7168, 4, 256], P('spec', None, 'gz'), may hold values from -6 to 6
Outputs:
- decrease: float32 [4096, 256], P('spec', 'gz')
- best: float32 [4096], P('spec')
Inputs may be any that keep to these rules, and one draw needn't show every extreme that they name: `mask`: 1 marks a good pixel, 0 a masked one.
All inputs are finite; a program needn't handle non-finite values. No bound on the sum of `mask` on one device may be relied on, other than what follows from the above.
Results may differ from a plain program's by a relative error of at most 0.0024.
Values may be sent and summed in bfloat16 or wider, within the bound.
A program may use at most 128 MiB of HBM per device.

v0:
```python
import jax
import jax.numpy as jnp
from jax import lax
from jax.sharding import PartitionSpec as P

PAIR_LIST = ((0, 0), (0, 1), (0, 2), (0, 3), (1, 1), (1, 2), (1, 3), (2, 2), (2, 3), (3, 3))


def pair_table(templates):
    columns = [
        templates[:, i, :].astype(jnp.float32) * templates[:, j, :].astype(jnp.float32)
        for i, j in PAIR_LIST
    ]
    return jnp.stack(columns, axis=1).astype(jnp.bfloat16)


def fit_gain(gram, proj):
    where = {}
    for number, pair in enumerate(PAIR_LIST):
        where[pair] = number
    lower = {}
    for j in range(4):
        diag = gram[:, where[j, j], :]
        for k in range(j):
            diag = diag - lower[j, k] * lower[j, k]
        lower[j, j] = jnp.sqrt(diag)
        for i in range(j + 1, 4):
            entry = gram[:, where[j, i], :]
            for k in range(j):
                entry = entry - lower[i, k] * lower[j, k]
            lower[i, j] = entry / lower[j, j]
    solved = []
    total = jnp.zeros(proj[:, 0, :].shape, jnp.float32)
    for i in range(4):
        value = proj[:, i, :]
        for k in range(i):
            value = value - lower[i, k] * solved[k]
        value = value / lower[i, i]
        solved.append(value)
        total = total + value * value
    return total


def local(flux, ivar, mask, table):
    ivar_f = ivar.astype(jnp.float32)
    mask_f = mask.astype(jnp.float32)
    weight = (ivar_f * mask_f).astype(jnp.bfloat16)
    weighted = (flux.astype(jnp.float32) * ivar_f * mask_f).astype(jnp.bfloat16)
    spectra_here = flux.shape[0]
    zlocal = table.shape[2]
    full_weighted, full_weight = (
        lax.all_gather(weighted, "gz", axis=1, tiled=True),
        lax.all_gather(weight, "gz", axis=1, tiled=True),
    )
    piece = lax.all_gather(table, "spec", axis=0, tiled=True)
    rows = piece.shape[0]
    flat_piece = piece.reshape(rows, 4 * zlocal)
    flat_pairs = pair_table(piece).reshape(rows, 10 * zlocal)
    proj = jnp.dot(full_weighted, flat_piece, preferred_element_type=jnp.float32)
    gram = jnp.dot(full_weight, flat_pairs, preferred_element_type=jnp.float32)
    proj = proj.reshape(spectra_here, 4, zlocal)
    gram = gram.reshape(spectra_here, 10, zlocal)
    decrease = fit_gain(gram, proj)
    best = lax.pmax(jnp.max(decrease, axis=1), "gz")
    return (decrease, best)


def solution(mesh):
    placed = (P("spec", "gz"), P("spec", "gz"), P("spec", "gz"), P("spec", None, "gz"))
    return jax.shard_map(
        local, mesh=mesh, in_specs=placed, out_specs=(P("spec", "gz"), P("spec")), check_vma=False
    )
```

profile of v0, /device:TPU:0, one launch (start us, length us, event | category | flops | bytes accessed | tf_op | source)
XLA Modules:
  0.0 207.5 jit_solution(3597575444971107315)
XLA Ops:
  7.2 0.0 all-gather.6.cloned.1.call-start
  7.2 0.7 all-gather.6.cloned.1.call-update
  7.9 0.0 all-gather.4.cloned.1.call-start
  7.9 5.8 %fusion.5 = (bf16[256,3584]{1,0:T(8,128)(2,1)}, bf16[256,3584]{1,0:T(8,128)(2,1)}) fusion(bf16[256,3584]{1,0:T(8,128)(2,1)} %param.5, s32[256,3584]{1,0:T(8,128)} %param.6, bf16[256,3584]{1,0:T(8,128)(2,1)} %param.4), kind=kLoop, calls=%fused_computation.17 | loop fusion | flops 7340032 | bytes 11010048 | tf_op jit(solution)/shard_map/convert_element_type | solution.py:48
  13.8 0.0 all-gather.4.cloned.1.call-update
  13.8 0.0 all-gather.8.cloned.1.call-start
  13.8 0.7 all-gather.8.cloned.1.call-update
  14.5 66.8 %all-gather.6.cloned.1.call-done = bf16[7168,4,128]{2,1,0:T(4,128)(2,1)} async-done(((bf16[448,4,128]{2,1,0:T(4,128)(2,1)}), bf16[7168,4,128]{2,1,0:T(4,128)(2,1)}) %all-gather.6.cloned.1.call-update) | async-done | bytes 7340048 | tf_op jit(solution)/shard_map/all_gather | solution.py:55
  81.3 12.5 %copy.17 = bf16[7168,4,128]{0,2,1:T(8,128)(2,1)} copy(bf16[7168,4,128]{2,1,0:T(4,128)(2,1)} %all-gather.6.cloned.1.call-done) | data formatting | bytes 14680064 | tf_op jit(solution)/shard_map/reshape | solution.py:57
  93.8 0.0 copy-start
  93.8 3.2 %fusion.28 = bf16[7168,10,128]{0,2,1:T(8,128)(2,1)} fusion(bf16[7168,4,128]{0,2,1:T(8,128)(2,1)} %copy.17), kind=kLoop, calls=%fused_computation.40 | loop fusion | flops 2752511 | bytes 3670016
  97.0 3.8 %fusion.27 = bf16[7168,10,128]{0,2,1:T(8,128)(2,1)} fusion(bf16[7168,10,128]{0,2,1:T(8,128)(2,1)} %fusion.28, bf16[7168,4,128]{0,2,1:T(8,128)(2,1)} %copy.17), kind=kLoop, calls=%fused_computation.39 | loop fusion | flops 3670016 | bytes 5505024
  100.8 0.0 copy-done
  100.8 1.7 fusion.25
  102.5 1.7 fusion.22
  104.2 1.7 fusion.26
  105.8 1.7 fusion.24
  107.5 1.7 fusion.21
  109.2 1.6 fusion.23
  110.8 21.4 %all-gather.4.cloned.1.call-done = bf16[256,7168]{1,0:T(8,128)(2,1)} async-done(((bf16[256,3584]{1,0:T(8,128)(2,1)}), bf16[256,7168]{1,0:T(8,128)(2,1)}) %all-gather.4.cloned.1.call-update) | async-done | bytes 3670032 | tf_op jit(solution)/shard_map/all_gather | solution.py:52
  132.1 6.3 %fusion.2 = f32[256,4,128]{0,2,1:T(8,128)S(1)} fusion(bf16[7168,4,128]{0,2,1:T(8,128)(2,1)} %copy.17, bf16[256,7168]{1,0:T(8,128)(2,1)} %all-gather.4.cloned.1.call-done), kind=kOutput, calls=%fused_computation.2 | convolution fusion | flops 1879048192 | bytes 11534336 | tf_op jit(solution)/shard_map/dot_general | solution.py:59
  138.4 4.1 %fusion.20 = bf16[7168,10,128]{0,2,1:T(8,128)(2,1)} fusion(bf16[7168,10,128]{0,2,1:T(8,128)(2,1)} %fusion.23, bf16[7168,4,128]{0,2,1:T(8,128)(2,1)} %copy.17), kind=kLoop, calls=%fused_computation.32 | loop fusion | flops 3670016 | bytes 5505024
  142.5 3.2 %fusion.19 = bf16[7168,10,128]{0,2,1:T(8,128)(2,1)} fusion(bf16[7168,10,128]{0,2,1:T(8,128)(2,1)} %fusion.20, bf16[7168,4,128]{0,2,1:T(8,128)(2,1)} %copy.17), kind=kLoop, calls=%fused_computation.31 | loop fusion | flops 2752512 | bytes 3670016 | tf_op jit(solution)/shard_map/stack | solution.py:14
  145.7 38.8 %all-gather.8.cloned.1.call-done = bf16[256,7168]{1,0:T(8,128)(2,1)} async-done(((bf16[256,3584]{1,0:T(8,128)(2,1)}), bf16[256,7168]{1,0:T(8,128)(2,1)}) %all-gather.8.cloned.1.call-update) | async-done | bytes 3670032 | tf_op jit(solution)/shard_map/all_gather | solution.py:53
  184.6 9.8 %fusion = f32[256,10,128]{0,2,1:T(8,128)S(1)} fusion(bf16[7168,10,128]{0,2,1:T(8,128)(2,1)} %fusion.19, bf16[256,7168]{1,0:T(8,128)(2,1)} %all-gather.8.cloned.1.call-done), kind=kOutput, calls=%fused_computation | convolution fusion | flops 4697620480 | bytes 23330816 | tf_op jit(solution)/shard_map/dot_general | solution.py:60
  194.4 0.4 fusion.47
  194.8 0.8 copy.16
  195.5 5.5 %pmax.7 = f32[256]{0:T(256)} all-reduce(f32[256]{0:T(256)S(1)} %get-tuple-element.8), channel_id=1, replica_groups=mesh['gz'=2,'spec'=16] {'gz'}, use_global_device_ids=true, to_apply=%region_1.0 | all-reduce | flops 256 | bytes 2048 | tf_op jit(solution)/shard_map/pmax | solution.py:64
Async XLA Ops:
  7.2 74.1 %all-gather.6.cloned.1.call-start = ((), (), s32[]{:S(2)}) async-start(), calls=%async_computation.1 | async-start | bytes 7798784 | tf_op jit(solution)/shard_map/all_gather | solution.py:55
  7.9 124.2 %all-gather.4.cloned.1.call-start = ((), (), s32[]{:S(2)}) async-start(), calls=%async_computation | async-start | bytes 5505024 | tf_op jit(solution)/shard_map/all_gather | solution.py:52
  13.8 170.8 %all-gather.8.cloned.1.call-start = ((), (), s32[]{:S(2)}) async-start(), calls=%async_computation.2 | async-start | bytes 5505024 | tf_op jit(solution)/shard_map/all_gather | solution.py:53
  93.8 7.0 %copy-start = (bf16[7168,4,128]{0,2,1:T(8,128)(2,1)S(1)}, bf16[7168,4,128]{0,2,1:T(8,128)(2,1)}, u32[]{:S(2)}) copy-start(bf16[7168,4,128]{0,2,1:T(8,128)(2,1)} %copy.17) | copy-start | bytes 22020100
Sparse Core Ops, SparseCore 0:
  10.3 70.9 all-gather.5
  82.8 49.2 all-gather.3
  133.7 50.8 all-gather.7
where the time goes:
time: 208 us
  waiting for transfers between devices  128 us (62%)
  other arithmetic  30.5 us (15%)
  matrix products  16.1 us (8%)
  between operations  13.8 us (7%)
  local copies, waits for them, and re-layouts  13.2 us (6%)
  blocking collectives  5.47 us (3%)
    all_gather x1, waiting for transfers between devices, local(): piece = lax.all_gather(table, 'spec', axis=0, tiled=True)  66.8 us
    all_gather x1, waiting for transfers between devices, local(): lax.all_gather(weight, 'gz', axis=1, tiled=True)  38.8 us
    all_gather x1, waiting for transfers between devices, local(): lax.all_gather(weighted, 'gz', axis=1, tiled=True)  21.4 us
    unnamed x9, other arithmetic  21.1 us
    reshape x1, local copies, waits for them, and re-layouts, local(): flat_piece = piece.reshape(rows, 4 * zlocal)  12.5 us
    dot_general x1, matrix products, local(): gram = jnp.dot(full_weight, flat_pairs, preferred_element_type=jnp.float32)  9.85 us
    dot_general x1, matrix products, local(): jnp.dot(full_weighted, flat_piece, preferred_element_type=jnp.float32)  6.3 us
    convert_element_type x1, other arithmetic, local(): weighted = (flux.astype(jnp.float32) * ivar_f * mask_f).astype(jnp.bfloat16)  5.81 us
  transfers between devices with their start and end apart: 3, of which 3 were waited for; matrix products, arithmetic and copies ran while one was open for 24% of the time, Pallas kernels for 0%

commit v1 on v0

v1 whole, which is shorter than its diff:
```python
import functools

import jax
import jax.numpy as jnp
from jax import lax
from jax.experimental import pallas as pl
from jax.experimental.pallas import tpu as pltpu
from jax.sharding import PartitionSpec as P

PAIR_LIST = ((0, 0), (0, 1), (0, 2), (0, 3), (1, 1), (1, 2), (1, 3), (2, 2), (2, 3), (3, 3))
MESH = pl.DeviceIdType.MESH
COMP = 4

STEPS = ((0, 0), (1, 0), (1, 1), (1, 2), (1, 3), (0, 1), (0, 2), (0, 3))


def pair_table(templates):
    columns = [
        templates[:, i, :].astype(jnp.float32) * templates[:, j, :].astype(jnp.float32)
        for i, j in PAIR_LIST
    ]
    return jnp.stack(columns, axis=1).astype(jnp.bfloat16)


def fit_gain(gram, proj):
    lower, inverse, solved, total = {}, [], [], None
    for j in range(COMP):
        diag = gram[j, j]
        for k in range(j):
            diag = diag - lower[j, k] * lower[j, k]
        inverse.append(lax.rsqrt(diag))
        for i in range(j + 1, COMP):
            entry = gram[j, i]
            for k in range(j):
                entry = entry - lower[i, k] * lower[j, k]
            lower[i, j] = entry * inverse[j]
        value = proj[j]
        for k in range(j):
            value = value - lower[j, k] * solved[k]
        value = value * inverse[j]
        solved.append(value)
        total = value * value if total is None else total + value * value
    return total


def gathered(flux, ivar, mask, table):
    ivar_f = ivar.astype(jnp.float32)
    mask_f = mask.astype(jnp.float32)
    weight = (ivar_f * mask_f).astype(jnp.bfloat16)
    weighted = (flux.astype(jnp.float32) * ivar_f * mask_f).astype(jnp.bfloat16)
    spectra_here = flux.shape[0]
    zlocal = table.shape[2]
    full_weighted = lax.all_gather(weighted, "gz", axis=1, tiled=True)
    full_weight = lax.all_gather(weight, "gz", axis=1, tiled=True)
    piece = lax.all_gather(table, "spec", axis=0, tiled=True)
    rows = piece.shape[0]
    flat_pairs = pair_table(piece).reshape(rows, 10 * zlocal)
    proj = jnp.dot(full_weighted, piece.reshape(rows, 4 * zlocal), preferred_element_type=jnp.float32)
    gram = jnp.dot(full_weight, flat_pairs, preferred_element_type=jnp.float32)
    proj = proj.reshape(spectra_here, 4, zlocal)
    gram = gram.reshape(spectra_here, 10, zlocal)
    decrease = fit_gain({p: gram[:, n] for n, p in enumerate(PAIR_LIST)}, [proj[:, k] for k in range(COMP)])
    return decrease, lax.pmax(jnp.max(decrease, axis=1), "gz")


def kernel(flux, ivar, mask, table, dec_ref, best_ref,
           flux_v, ivar_v, mask_v, weight, weighted, tbuf, pairs, gram_own, proj_own,
           gram_send, proj_send, gram_recv, proj_recv, top_send, top_recv,
           in_sem, recv_sem, up_sem, down_sem, x_sem, sib_sem, y_sem,
           part_send, part_recv, top_sems):
    y, s = lax.axis_index("gz"), lax.axis_index("spec")
    z, x, c = s // 4, lax.rem(s // 2, 2), lax.rem(s, 2)
    u = jnp.where(y == 0, z, 3 - z)
    dz = 1 - 2 * y
    spectra, waves = flux.shape
    blocks = tbuf.shape[2]

    def at(zz, xx, cc):
        return zz * 4 + xx * 2 + cc

    partner = (1 - y, s)
    sibling = (y, at(z, x, 1 - c))
    across = (y, at(z, 1 - x, c))
    up = (y, at(z + dz, x, c))
    down = (y, at(z - dz, x, c))

    loads = [
        pltpu.make_async_copy(ref, buf, in_sem.at[n])
        for n, (ref, buf) in enumerate(((flux, flux_v), (ivar, ivar_v), (mask, mask_v)))
    ]

    mine = at(z - 2 * y, x, c)
    theirs = at(z - 2 * (1 - y), x, c)

    def own_copy(k):
        return pltpu.make_async_copy(table.at[k], tbuf.at[0, k, mine], recv_sem.at[k, mine])

    def y_copy(k):
        return pltpu.make_async_remote_copy(
            src_ref=table.at[k], dst_ref=tbuf.at[1, k, theirs], send_sem=y_sem.at[k],
            recv_sem=recv_sem.at[COMP + k, theirs], device_id=partner, device_id_type=MESH)

    @pl.when(u <= 1)
    def _():
        for k in range(COMP):
            own_copy(k).start()

    barrier = pltpu.get_barrier_semaphore()
    for other in (partner, sibling, across):
        pl.semaphore_signal(barrier, inc=1, device_id=other, device_id_type=MESH)

    @pl.when(u <= 2)
    def _():
        pl.semaphore_signal(barrier, inc=1, device_id=up, device_id_type=MESH)

    @pl.when(u >= 1)
    def _():
        pl.semaphore_signal(barrier, inc=1, device_id=down, device_id_type=MESH)

    for load in loads:
        load.start()
    pl.semaphore_wait(barrier, jnp.where((u == 0) | (u == 3), 4, 5))

    @pl.when(u >= 2)
    def _():
        for k in range(COMP):
            y_copy(k).start()

    first = jnp.where(u >= 1, 1, 0)

    def block(j, xx, cc):
        v = first if j == 0 else 1 - first
        zrel = jnp.where(y == 0, v, 1 - v)
        return at(zrel, xx, cc)

    def arrived(t, b):
        w, k = STEPS[t]
        slot = tbuf.at[w, k, b]
        pltpu.make_async_copy(slot, slot, recv_sem.at[w * COMP + k, b]).wait()

    def forward(t, b, send_sem, to):
        w, k = STEPS[t]
        return pltpu.make_async_remote_copy(
            src_ref=tbuf.at[w, k, b], dst_ref=tbuf.at[w, k, b], send_sem=send_sem,
            recv_sem=recv_sem.at[w * COMP + k, b], device_id=to, device_id_type=MESH)

    def column_sends(t, j, do):
        b = block(j, x, c)

        @pl.when((u <= 2) if j == 0 else ((u == 1) | (u == 2)))
        def _():
            do(forward(t, b, up_sem.at[t, j], up))

        do(forward(t, b, x_sem.at[t, j], across))
        if j == 0:
            @pl.when(u == 1)
            def _():
                do(forward(t, b, down_sem.at[t], down))
        do(forward(t, b, sib_sem.at[t, j], sibling))

    def across_sends(t, j, do):
        do(forward(t, block(j, 1 - x, c), sib_sem.at[t, 2 + j], sibling))

    def column(t):
        for j in range(2):
            arrived(t, block(j, x, c))
            column_sends(t, j, lambda copy: copy.start())

    def neighbour(t):
        for j in range(2):
            arrived(t, block(j, 1 - x, c))
            across_sends(t, j, lambda copy: copy.start())

    def weights():
        for load in loads:
            load.wait()
        step = 32

        def body(n, carry):
            rows = pl.ds(pl.multiple_of(n * step, step), step)
            iv = ivar_v[rows, :].astype(jnp.float32)
            mk = mask_v[rows, :].astype(jnp.float32)
            weight[rows, :] = (iv * mk).astype(jnp.bfloat16)
            weighted[rows, :] = (flux_v[rows, :].astype(jnp.float32) * iv * mk).astype(jnp.bfloat16)
            return carry

        lax.fori_loop(0, spectra // step, body, 0)

    def part_copies(k):
        low = k * (k + 1) // 2
        refs = ((proj_send, proj_recv, pl.ds(k, 1)), (gram_send, gram_recv, pl.ds(low, k + 1)))
        return [
            pltpu.make_async_remote_copy(
                src_ref=src.at[rows], dst_ref=dst.at[rows], send_sem=part_send.at[k, n],
                recv_sem=part_recv.at[k, n], device_id=partner, device_id_type=MESH)
            for n, (src, dst, rows) in enumerate(refs)
        ]

    def compute(t):
        w, k = STEPS[t]
        for xx in range(2):
            for j in range(2):
                arrived(t, block(j, xx, 1 - c))
        for b in range(blocks):
            depth = tbuf.shape[3]
            rows = slice(b * depth, (b + 1) * depth)
            for i in range(k + 1):
                pairs[rows, i * 128:(i + 1) * 128] = tbuf[w, i, b] * tbuf[w, k, b]
        zlocal = tbuf.shape[4]
        proj = jnp.dot(weighted[...], tbuf[w, k].reshape(waves, zlocal), preferred_element_type=jnp.float32)
        gram = jnp.dot(weight[...], pairs[:, : (k + 1) * 128], preferred_element_type=jnp.float32)
        low = k * (k + 1) // 2
        if w == 0:
            proj_own[k] = proj
        else:
            proj_send[k] = proj
        for i in range(k + 1):
            part = gram[:, i * 128:(i + 1) * 128]
            if w == 0:
                gram_own[low + i] = part
            else:
                gram_send[low + i] = part.astype(jnp.bfloat16)
        if w == 1:
            for copy in part_copies(k):
                copy.start()

    count = len(STEPS)
    column(0)
    column(1)
    neighbour(0)
    weights()
    compute(0)
    for t in range(2, count):
        column(t)
        neighbour(t - 1)
        compute(t - 1)
    neighbour(count - 1)
    compute(count - 1)

    for k in range(COMP):
        for copy in part_copies(k):
            copy.wait_recv()
    step = 64

    def solve(n, carry):
        rows = pl.ds(pl.multiple_of(n * step, step), step)
        gram, proj = {}, []
        for k in range(COMP):
            proj.append(proj_own[k, rows, :] + proj_recv[k, rows, :])
            for i in range(k + 1):
                m = k * (k + 1) // 2 + i
                gram[i, k] = gram_own[m, rows, :] + gram_recv[m, rows, :].astype(jnp.float32)
        dec_ref[rows, :] = fit_gain(gram, proj)
        return carry

    lax.fori_loop(0, spectra // step, solve, 0)
    top = jnp.max(dec_ref[...].T, axis=0, keepdims=True)
    top_send[...] = jnp.broadcast_to(top, top_send.shape)
    top_copy = pltpu.make_async_remote_copy(
        src_ref=top_send, dst_ref=top_recv, send_sem=top_sems.at[0], recv_sem=top_sems.at[1],
        device_id=partner, device_id_type=MESH)
    top_copy.start()

    @pl.when(u >= 2)
    def _():
        for k in range(COMP):
            y_copy(k).wait_send()

    for t in range(count):
        for j in range(2):
            column_sends(t, j, lambda copy: copy.wait_send())
            across_sends(t, j, lambda copy: copy.wait_send())
    for k in range(COMP):
        for copy in part_copies(k):
            copy.wait_send()
    top_copy.wait()
    best_ref[...] = jnp.maximum(top_send[...], top_recv[...])


def fused(flux, ivar, mask, table):
    spectra, waves = flux.shape
    depth, comp, zlocal = table.shape
    pieces = comp * (comp + 1) // 2
    blocks = waves // depth
    by_component = table.transpose(1, 0, 2)
    bf16, f32 = jnp.bfloat16, jnp.float32
    dma = pltpu.SemaphoreType.DMA
    steps = len(STEPS)
    decrease, best = pl.pallas_call(
        kernel,
        out_shape=(
            jax.ShapeDtypeStruct((spectra, zlocal), f32),
            jax.ShapeDtypeStruct((8, spectra), f32),
        ),
        in_specs=[pl.BlockSpec(memory_space=pl.ANY)] * 4,
        out_specs=(pl.BlockSpec(memory_space=pltpu.VMEM), pl.BlockSpec(memory_space=pltpu.VMEM)),
        scratch_shapes=[
            pltpu.VMEM((spectra, waves), flux.dtype),
            pltpu.VMEM((spectra, waves), ivar.dtype),
            pltpu.VMEM((spectra, waves), mask.dtype),
            pltpu.VMEM((spectra, waves), bf16),
            pltpu.VMEM((spectra, waves), bf16),
            pltpu.VMEM((2, comp, blocks, depth, zlocal), bf16),
            pltpu.VMEM((waves, comp * zlocal), bf16),
            pltpu.VMEM((pieces, spectra, zlocal), f32),
            pltpu.VMEM((comp, spectra, zlocal), f32),
            pltpu.VMEM((pieces, spectra, zlocal), bf16),
            pltpu.VMEM((comp, spectra, zlocal), f32),
            pltpu.VMEM((pieces, spectra, zlocal), bf16),
            pltpu.VMEM((comp, spectra, zlocal), f32),
            pltpu.VMEM((8, spectra), f32),
            pltpu.VMEM((8, spectra), f32),
            dma((3,)),
            dma((steps, blocks)),
            dma((steps, 2)),
            dma((steps,)),
            dma((steps, 2)),
            dma((steps, 4)),
            dma((comp,)),
            dma((comp, 2)),
            dma((comp, 2)),
            dma((2,)),
        ],
        compiler_params=pltpu.CompilerParams(
            collective_id=0, has_side_effects=True, vmem_limit_bytes=48 * 1024 * 1024
        ),
        cost_estimate=pl.CostEstimate(
            flops=2 * spectra * waves * 2 * zlocal * (comp + pieces),
            bytes_accessed=8 * spectra * waves, transcendentals=0),
    )(flux, ivar, mask, by_component)
    return decrease, best[0]


def solution(mesh):
    placed = (P("spec", "gz"), P("spec", "gz"), P("spec", "gz"), P("spec", None, "gz"))
    local = fused if (mesh.shape["gz"], mesh.shape["spec"]) == (2, 16) else gathered
    return jax.shard_map(
        local, mesh=mesh, in_specs=placed, out_specs=(P("spec", "gz"), P("spec")), check_vma=False
    )
```

time: 208 us -> 84.9 us (0.41)
  waiting for transfers between devices: 128 us -> 0 us
  Pallas kernels: 0 us -> 78.8 us
  other arithmetic: 30.5 us -> 0 us
  matrix products: 16.1 us -> 0 us
  between operations: 13.8 us -> 0.65 us
  local copies, waits for them, and re-layouts: 13.2 us -> 5.29 us
  blocking collectives: 5.47 us -> 0 us
    all_gather x3 -> x0, waiting for transfers between devices: 127 us -> none  [the longest x1 66.8 us: local(): piece = lax.all_gather(table, 'spec', axis=0, tiled=True)]
    pallas_call x0 -> x1, Pallas kernels: none -> 78.8 us  [fused(): pl.pallas_call(kernel, out_shape=(jax.ShapeDtypeStruct((spectra, zlocal),...]
    unnamed x9 -> x0, other arithmetic: 21.1 us -> none
    dot_general x2 -> x0, matrix products: 16.1 us -> none  [the longest x1 9.85 us: local(): gram = jnp.dot(full_weight, flat_pairs, preferred_element_type=jnp.float32)]
    reshape x1 -> x0, local copies, waits for them, and re-layouts: 12.5 us -> none  [local(): flat_piece = piece.reshape(rows, 4 * zlocal)]
    convert_element_type x1 -> x0, other arithmetic: 5.81 us -> none  [local(): weighted = (flux.astype(jnp.float32) * ivar_f * mask_f).astype(jnp.bfloat16)]
    pmax x1 -> x0, blocking collectives: 5.47 us -> none  [local(): best = lax.pmax(jnp.max(decrease, axis=1), 'gz')]
    unnamed x3 -> x6, local copies, waits for them, and re-layouts: 0.76 us -> 4.73 us
  transfers between devices with their start and end apart: 3 -> 0, of which waited for: 3 -> 0; matrix products, arithmetic and copies ran while one was open for 24% -> 0% of each run, Pallas kernels for 0% -> 0%
where the time goes in v1:
time: 84.9 us; the launch traced here: 84.7 us
  Pallas kernels  78.8 us (93%)
  local copies, waits for them, and re-layouts  5.29 us (6%)
    pallas_call x1, Pallas kernels, fused(): pl.pallas_call(kernel, out_shape=(jax.ShapeDtypeStruct((spectra, zlocal),...  78.8 us
    unnamed x6, local copies, waits for them, and re-layouts  4.73 us

profile of v1, /device:TPU:0, one launch (start us, length us, event | category | flops | bytes accessed | tf_op | source)
XLA Modules:
  0.0 84.7 jit_solution(1226052044506159683)
XLA Ops:
  0.6 1.1 %copy.8 = bf16[448,4,128]{2,0,1:T(8,128)(2,1)S(1)} copy(bf16[448,4,128]{2,1,0:T(4,128)(2,1)} %param.7) | data formatting | bytes 917504 | tf_op args[3]
  1.7 0.0 copy-start
  1.7 1.5 %copy-done = bf16[256,3584]{1,0:T(8,128)(2,1)S(1)} copy-done((bf16[256,3584]{1,0:T(8,128)(2,1)S(1)}, bf16[256,3584]{1,0:T(8,128)(2,1)}, u32[]{:S(2)}) %copy-start) | copy-done | bytes 1835032
  3.2 0.0 copy-start.1
  3.2 1.5 %copy-done.1 = bf16[256,3584]{1,0:T(8,128)(2,1)S(1)} copy-done((bf16[256,3584]{1,0:T(8,128)(2,1)S(1)}, bf16[256,3584]{1,0:T(8,128)(2,1)}, u32[]{:S(2)}) %copy-start.1) | copy-done | bytes 1835032
  4.7 78.8 %shard_map.59 = (f32[256,128]{1,0:T(8,128)S(1)}, f32[8,256]{1,0:T(8,128)S(1)}) custom-call(bf16[256,3584]{1,0:T(8,128)(2,1)S(1)} %copy-done, bf16[256,3584]{1,0:T(8,128)(2,1)S(1)} %copy-done.1, s32[256,3584]{1,0:T(8,128)} %mask.1, bf16[4,448,128]{2,1,0:T(8,128)(2,1)S(1)} %bitcast.4), custom_call_target="tpu_custom_call" | custom-call | flops 6576668672 | bytes 7340032 | tf_op jit(solution)/shard_map/pallas_call | solution.py:289
  83.5 0.6 slice.3
  84.1 0.7 copy.10
Async XLA Ops:
  1.7 1.5 %copy-start = (bf16[256,3584]{1,0:T(8,128)(2,1)S(1)}, bf16[256,3584]{1,0:T(8,128)(2,1)}, u32[]{:S(2)}) copy-start(bf16[256,3584]{1,0:T(8,128)(2,1)} %flux.1) | copy-start | bytes 5505028
  3.2 1.5 %copy-start.1 = (bf16[256,3584]{1,0:T(8,128)(2,1)S(1)}, bf16[256,3584]{1,0:T(8,128)(2,1)}, u32[]{:S(2)}) copy-start(bf16[256,3584]{1,0:T(8,128)(2,1)} %ivar.1) | copy-start | bytes 5505028

commit v2 on v1

--- a/solution.py
+++ b/solution.py
@@ -121,12 +121,16 @@
         load.start()
     pl.semaphore_wait(barrier, jnp.where((u == 0) | (u == 3), 4, 5))
 
-    @pl.when(u >= 2)
-    def _():
-        for k in range(COMP):
-            y_copy(k).start()
+    def y_start(*which):
+        @pl.when(u >= 2)
+        def _():
+            for k in which:
+                y_copy(k).start()
+
+    y_start(0, 1)
 
     first = jnp.where(u >= 1, 1, 0)
+    count = len(STEPS)
 
     def block(j, xx, cc):
         v = first if j == 0 else 1 - first
@@ -161,13 +165,13 @@
     def across_sends(t, j, do):
         do(forward(t, block(j, 1 - x, c), sib_sem.at[t, 2 + j], sibling))
 
-    def column(t):
-        for j in range(2):
+    def column(t, j):
+        if 0 <= t < count:
             arrived(t, block(j, x, c))
             column_sends(t, j, lambda copy: copy.start())
 
-    def neighbour(t):
-        for j in range(2):
+    def neighbour(t, j):
+        if 0 <= t < count:
             arrived(t, block(j, 1 - x, c))
             across_sends(t, j, lambda copy: copy.start())
 
@@ -196,46 +200,57 @@
             for n, (src, dst, rows) in enumerate(refs)
         ]
 
-    def compute(t):
+    def compute(t, stage):
+        if not 0 <= t < count:
+            return
         w, k = STEPS[t]
-        for xx in range(2):
-            for j in range(2):
-                arrived(t, block(j, xx, 1 - c))
-        for b in range(blocks):
-            depth = tbuf.shape[3]
-            rows = slice(b * depth, (b + 1) * depth)
-            for i in range(k + 1):
-                pairs[rows, i * 128:(i + 1) * 128] = tbuf[w, i, b] * tbuf[w, k, b]
-        zlocal = tbuf.shape[4]
-        proj = jnp.dot(weighted[...], tbuf[w, k].reshape(waves, zlocal), preferred_element_type=jnp.float32)
-        gram = jnp.dot(weight[...], pairs[:, : (k + 1) * 128], preferred_element_type=jnp.float32)
+        depth, zlocal = tbuf.shape[3:]
         low = k * (k + 1) // 2
-        if w == 0:
-            proj_own[k] = proj
-        else:
-            proj_send[k] = proj
-        for i in range(k + 1):
-            part = gram[:, i * 128:(i + 1) * 128]
+        if stage == 0:
+            for xx in range(2):
+                for j in range(2):
+                    arrived(t, block(j, xx, 1 - c))
+        if stage < 2:
+            for i in range(stage, k + 1, 2):
+                for b in range(blocks):
+                    pairs[b * depth:(b + 1) * depth, i * zlocal:(i + 1) * zlocal] = tbuf[w, i, b] * tbuf[w, k, b]
+        if stage == 1:
+            proj = jnp.dot(weighted[...], tbuf[w, k].reshape(waves, zlocal), preferred_element_type=jnp.float32)
             if w == 0:
-                gram_own[low + i] = part
+                proj_own[k] = proj
             else:
-                gram_send[low + i] = part.astype(jnp.bfloat16)
-        if w == 1:
+                proj_send[k] = proj
+        if stage >= 2:
+            start = 2 * (stage - 2)
+            stop = min(start + 2, k + 1)
+            if start < stop:
+                gram = jnp.dot(
+                    weight[...], pairs[:, start * zlocal:stop * zlocal], preferred_element_type=jnp.float32)
+                for i in range(start, stop):
+                    part = gram[:, (i - start) * zlocal:(i - start + 1) * zlocal]
+                    if w == 0:
+                        gram_own[low + i] = part
+                    else:
+                        gram_send[low + i] = part.astype(jnp.bfloat16)
+        if stage == 3 and w == 1:
             for copy in part_copies(k):
                 copy.start()
 
-    count = len(STEPS)
-    column(0)
-    column(1)
-    neighbour(0)
-    weights()
-    compute(0)
-    for t in range(2, count):
-        column(t)
-        neighbour(t - 1)
-        compute(t - 1)
-    neighbour(count - 1)
-    compute(count - 1)
+    column(0, 0)
+    y_start(2)
+    for t in range(count + 2):
+        column(t + 1, 0)
+        if t == 0:
+            y_start(3)
+        compute(t - 2, 0)
+        column(t, 1)
+        compute(t - 2, 1)
+        neighbour(t, 0)
+        compute(t - 2, 2)
+        neighbour(t - 1, 1)
+        if t == 1:
+            weights()
+        compute(t - 2, 3)
 
     for k in range(COMP):
         for copy in part_copies(k):
@@ -274,7 +289,7 @@
         for copy in part_copies(k):
             copy.wait_send()
     top_copy.wait()
-    best_ref[...] = jnp.maximum(top_send[...], top_recv[...])
+    best_ref[...] = jnp.maximum(top_send[0:1, :], top_recv[0:1, :])
 
 
 def fused(flux, ivar, mask, table):
@@ -290,7 +305,7 @@
         kernel,
         out_shape=(
             jax.ShapeDtypeStruct((spectra, zlocal), f32),
-            jax.ShapeDtypeStruct((8, spectra), f32),
+            jax.ShapeDtypeStruct((1, spectra), f32),
         ),
         in_specs=[pl.BlockSpec(memory_space=pl.ANY)] * 4,
         out_specs=(pl.BlockSpec(memory_space=pltpu.VMEM), pl.BlockSpec(memory_space=pltpu.VMEM)),
@@ -322,13 +337,13 @@
             dma((2,)),
         ],
         compiler_params=pltpu.CompilerParams(
-            collective_id=0, has_side_effects=True, vmem_limit_bytes=48 * 1024 * 1024
+            collective_id=0, has_side_effects=True, vmem_limit_bytes=63 * 1024 * 1024
         ),
         cost_estimate=pl.CostEstimate(
             flops=2 * spectra * waves * 2 * zlocal * (comp + pieces),
             bytes_accessed=8 * spectra * waves, transcendentals=0),
     )(flux, ivar, mask, by_component)
-    return decrease, best[0]
+    return decrease, best.reshape(spectra)
 
 
 def solution(mesh):

time: 84.9 us -> 74.3 us (0.88)
  Pallas kernels: 78.8 us -> 68.8 us
    pallas_call x1, Pallas kernels: 78.8 us -> 68.8 us  [fused(): pl.pallas_call(kernel, out_shape=(jax.ShapeDtypeStruct((spectra, zlocal),...]
    unnamed x6 -> x3, local copies, waits for them, and re-layouts: 4.73 us -> 4.64 us
where the time goes in v2:
time: 74.3 us; the launch traced here: 74.1 us
  Pallas kernels  68.8 us (93%)
  local copies, waits for them, and re-layouts  4.64 us (6%)
    pallas_call x1, Pallas kernels, fused(): pl.pallas_call(kernel, out_shape=(jax.ShapeDtypeStruct((spectra, zlocal),...  68.8 us
    unnamed x3, local copies, waits for them, and re-layouts  4.64 us

profile of v2, /device:TPU:0, one launch (start us, length us, event | category | flops | bytes accessed | tf_op | source)
XLA Modules:
  0.0 74.1 jit_solution(1122705569206149920)
XLA Ops:
  0.6 1.8 %copy.8 = bf16[448,4,128]{2,0,1:T(8,128)(2,1)} copy(bf16[448,4,128]{2,1,0:T(4,128)(2,1)} %param.7) | data formatting | bytes 917504 | tf_op args[3]
  2.5 68.8 %shard_map.59 = (f32[256,128]{1,0:T(8,128)}, f32[1,256]{1,0:T(1,128)}) custom-call(bf16[256,3584]{1,0:T(8,128)(2,1)} %flux.1, bf16[256,3584]{1,0:T(8,128)(2,1)} %ivar.1, s32[256,3584]{1,0:T(8,128)} %mask.1, bf16[4,448,128]{2,1,0:T(8,128)(2,1)} %bitcast.4), custom_call_target="tpu_custom_call" | custom-call | flops 6576668672 | bytes 7340032 | tf_op jit(solution)/shard_map/pallas_call | solution.py:304
  71.3 1.6 %copy.11 = f32[256,128]{1,0:T(8,128)} copy(f32[256,128]{1,0:T(8,128)} %get-tuple-element.8) | data formatting | bytes 262144
  72.9 1.2 %copy.12 = f32[256]{0:T(256)} copy(f32[256]{0:T(256)} %bitcast.5) | data formatting | bytes 2048

commit v3 on v2

--- a/solution.py
+++ b/solution.py
@@ -12,6 +12,7 @@
 COMP = 4
 
 STEPS = ((0, 0), (1, 0), (1, 1), (1, 2), (1, 3), (0, 1), (0, 2), (0, 3))
+LAST_PARTS = 4
 
 
 def pair_table(templates):
@@ -92,8 +93,22 @@
     mine = at(z - 2 * y, x, c)
     theirs = at(z - 2 * (1 - y), x, c)
 
-    def own_copy(k):
-        return pltpu.make_async_copy(table.at[k], tbuf.at[0, k, mine], recv_sem.at[k, mine])
+    count = len(STEPS)
+    depth, zlocal = tbuf.shape[3:]
+
+    def parts(w, k):
+        return range(LAST_PARTS if (w, k) == STEPS[-1] else 1)
+
+    def part_of(w, k, q):
+        size = depth // len(parts(w, k))
+        return pl.ds(q * size, size)
+
+    def landed(w, k, b, q):
+        return recv_sem.at[w * COMP + k if q == 0 else 2 * COMP + q - 1, b]
+
+    def own_copy(k, q):
+        rows = part_of(0, k, q)
+        return pltpu.make_async_copy(table.at[k, rows], tbuf.at[0, k, mine, rows], landed(0, k, mine, q))
 
     def y_copy(k):
         return pltpu.make_async_remote_copy(
@@ -103,7 +118,8 @@
     @pl.when(u <= 1)
     def _():
         for k in range(COMP):
-            own_copy(k).start()
+            for q in parts(0, k):
+                own_copy(k, q).start()
 
     barrier = pltpu.get_barrier_semaphore()
     for other in (partner, sibling, across):
@@ -130,55 +146,61 @@
     y_start(0, 1)
 
     first = jnp.where(u >= 1, 1, 0)
-    count = len(STEPS)
+
+    def half(j):
+        v = first if j == 0 else 1 - first
+        return jnp.where(y == 0, v, 1 - v)
 
     def block(j, xx, cc):
-        v = first if j == 0 else 1 - first
-        zrel = jnp.where(y == 0, v, 1 - v)
-        return at(zrel, xx, cc)
-
-    def arrived(t, b):
+        return at(half(j), xx, cc)
+
+    def arrived(t, b, q):
         w, k = STEPS[t]
-        slot = tbuf.at[w, k, b]
-        pltpu.make_async_copy(slot, slot, recv_sem.at[w * COMP + k, b]).wait()
-
-    def forward(t, b, send_sem, to):
+        slot = tbuf.at[w, k, b, part_of(w, k, q)]
+        pltpu.make_async_copy(slot, slot, landed(w, k, b, q)).wait()
+
+    def forward(t, b, q, send_sem, to):
         w, k = STEPS[t]
+        slot = tbuf.at[w, k, b, part_of(w, k, q)]
         return pltpu.make_async_remote_copy(
-            src_ref=tbuf.at[w, k, b], dst_ref=tbuf.at[w, k, b], send_sem=send_sem,
-            recv_sem=recv_sem.at[w * COMP + k, b], device_id=to, device_id_type=MESH)
-
-    def column_sends(t, j, do):
-        b = block(j, x, c)
+            src_ref=slot, dst_ref=slot, send_sem=send_sem, recv_sem=landed(w, k, b, q),
+            device_id=to, device_id_type=MESH)
+
+    def column_sends(t, j, q, do):
+        b, n = block(j, x, c), t + q
 
         @pl.when((u <= 2) if j == 0 else ((u == 1) | (u == 2)))
         def _():
-            do(forward(t, b, up_sem.at[t, j], up))
-
-        do(forward(t, b, x_sem.at[t, j], across))
+            do(forward(t, b, q, up_sem.at[n, j], up))
+
+        do(forward(t, b, q, x_sem.at[n, j], across))
         if j == 0:
             @pl.when(u == 1)
             def _():
-                do(forward(t, b, down_sem.at[t], down))
-        do(forward(t, b, sib_sem.at[t, j], sibling))
-
-    def across_sends(t, j, do):
-        do(forward(t, block(j, 1 - x, c), sib_sem.at[t, 2 + j], sibling))
+                do(forward(t, b, q, down_sem.at[n], down))
+        do(forward(t, b, q, sib_sem.at[n, j], sibling))
+
+    def across_sends(t, j, q, do):
+        do(forward(t, block(j, 1 - x, c), q, sib_sem.at[t + q, 2 + j], sibling))
 
     def column(t, j):
         if 0 <= t < count:
-            arrived(t, block(j, x, c))
-            column_sends(t, j, lambda copy: copy.start())
+            for q in parts(*STEPS[t]):
+                arrived(t, block(j, x, c), q)
+                column_sends(t, j, q, lambda copy: copy.start())
 
     def neighbour(t, j):
         if 0 <= t < count:
-            arrived(t, block(j, 1 - x, c))
-            across_sends(t, j, lambda copy: copy.start())
-
-    def weights():
-        for load in loads:
-            load.wait()
+            for q in parts(*STEPS[t]):
+                arrived(t, block(j, 1 - x, c), q)
+                across_sends(t, j, q, lambda copy: copy.start())
+
+    def weights(stage):
+        if stage == 0:
+            for load in loads:
+                load.wait()
         step = 32
+        some = spectra // step // 4
 
         def body(n, carry):
             rows = pl.ds(pl.multiple_of(n * step, step), step)
@@ -188,7 +210,7 @@
             weighted[rows, :] = (flux_v[rows, :].astype(jnp.float32) * iv * mk).astype(jnp.bfloat16)
             return carry
 
-        lax.fori_loop(0, spectra // step, body, 0)
+        lax.fori_loop(stage * some, (stage + 1) * some, body, 0)
 
     def part_copies(k):
         low = k * (k + 1) // 2
@@ -201,15 +223,16 @@
         ]
 
     def compute(t, stage):
-        if not 0 <= t < count:
+        if t == -1:
+            weights(stage)
+        if not 0 <= t < count - 1:
             return
         w, k = STEPS[t]
-        depth, zlocal = tbuf.shape[3:]
         low = k * (k + 1) // 2
         if stage == 0:
             for xx in range(2):
                 for j in range(2):
-                    arrived(t, block(j, xx, 1 - c))
+                    arrived(t, block(j, xx, 1 - c), 0)
         if stage < 2:
             for i in range(stage, k + 1, 2):
                 for b in range(blocks):
@@ -236,9 +259,30 @@
             for copy in part_copies(k):
                 copy.start()
 
+    def compute_last(j):
+        w, k = STEPS[-1]
+        low = k * (k + 1) // 2
+        for xx in range(2):
+            for q in parts(w, k):
+                arrived(count - 1, block(j, xx, 1 - c), q)
+        some, size = blocks // 2, waves // 2
+        base = half(j) * some
+        columns = pl.ds(pl.multiple_of(half(j) * size, 128), size)
+        for i in range(k + 1):
+            for n in range(some):
+                pairs[n * depth:(n + 1) * depth, i * zlocal:(i + 1) * zlocal] = (
+                    tbuf[w, i, base + n] * tbuf[w, k, base + n])
+        new = tbuf[w, k, pl.ds(base, some)].reshape(size, zlocal)
+        proj = jnp.dot(weighted[:, columns], new, preferred_element_type=jnp.float32)
+        proj_own[k] = proj if j == 0 else proj_own[k] + proj
+        gram = jnp.dot(weight[:, columns], pairs[:size, :(k + 1) * zlocal], preferred_element_type=jnp.float32)
+        for i in range(k + 1):
+            part = gram[:, i * zlocal:(i + 1) * zlocal]
+            gram_own[low + i] = part if j == 0 else gram_own[low + i] + part
+
     column(0, 0)
     y_start(2)
-    for t in range(count + 2):
+    for t in range(count):
         column(t + 1, 0)
         if t == 0:
             y_start(3)
@@ -248,9 +292,14 @@
         neighbour(t, 0)
         compute(t - 2, 2)
         neighbour(t - 1, 1)
-        if t == 1:
-            weights()
         compute(t - 2, 3)
+    compute(count - 2, 0)
+    compute(count - 2, 1)
+    neighbour(count - 1, 1)
+    compute(count - 2, 2)
+    compute(count - 2, 3)
+    compute_last(0)
+    compute_last(1)
 
     for k in range(COMP):
         for copy in part_copies(k):
@@ -283,8 +332,9 @@
 
     for t in range(count):
         for j in range(2):
-            column_sends(t, j, lambda copy: copy.wait_send())
-            across_sends(t, j, lambda copy: copy.wait_send())
+            for q in parts(*STEPS[t]):
+                column_sends(t, j, q, lambda copy: copy.wait_send())
+                across_sends(t, j, q, lambda copy: copy.wait_send())
     for k in range(COMP):
         for copy in part_copies(k):
             copy.wait_send()
@@ -326,18 +376,18 @@
             pltpu.VMEM((8, spectra), f32),
             pltpu.VMEM((8, spectra), f32),
             dma((3,)),
-            dma((steps, blocks)),
-            dma((steps, 2)),
-            dma((steps,)),
-            dma((steps, 2)),
-            dma((steps, 4)),
+            dma((2 * comp + LAST_PARTS - 1, blocks)),
+            dma((steps + LAST_PARTS - 1, 2)),
+            dma((steps + LAST_PARTS - 1,)),
+            dma((steps + LAST_PARTS - 1, 2)),
+            dma((steps + LAST_PARTS - 1, 4)),
             dma((comp,)),
             dma((comp, 2)),
             dma((comp, 2)),
             dma((2,)),
         ],
         compiler_params=pltpu.CompilerParams(
-            collective_id=0, has_side_effects=True, vmem_limit_bytes=63 * 1024 * 1024
+            collective_id=0, has_side_effects=True, vmem_limit_bytes=123 * 512 * 1024
         ),
         cost_estimate=pl.CostEstimate(
             flops=2 * spectra * waves * 2 * zlocal * (comp + pieces),

time: 74.3 us -> 73.8 us (level)
  Pallas kernels: 68.8 us -> 67.8 us
    pallas_call x1, Pallas kernels: 68.8 us -> 67.8 us  [fused(): pl.pallas_call(kernel, out_shape=(jax.ShapeDtypeStruct((spectra, zlocal),...]
where the time goes in v3:
time: 73.8 us; the launch traced here: 73.1 us
  Pallas kernels  67.8 us (92%)
  local copies, waits for them, and re-layouts  4.64 us (6%)
    pallas_call x1, Pallas kernels, fused(): pl.pallas_call(kernel, out_shape=(jax.ShapeDtypeStruct((spectra, zlocal),...  67.8 us
    unnamed x3, local copies, waits for them, and re-layouts  4.64 us

profile of v3, /device:TPU:0, one launch (start us, length us, event | category | flops | bytes accessed | tf_op | source)
XLA Modules:
  0.0 73.1 jit_solution(10671177159356707190)
XLA Ops:
  0.6 1.8 %copy.8 = bf16[448,4,128]{2,0,1:T(8,128)(2,1)} copy(bf16[448,4,128]{2,1,0:T(4,128)(2,1)} %param.7) | data formatting | bytes 917504 | tf_op args[3]
  2.5 67.8 %shard_map.59 = (f32[256,128]{1,0:T(8,128)}, f32[1,256]{1,0:T(1,128)}) custom-call(bf16[256,3584]{1,0:T(8,128)(2,1)} %flux.1, bf16[256,3584]{1,0:T(8,128)(2,1)} %ivar.1, s32[256,3584]{1,0:T(8,128)} %mask.1, bf16[4,448,128]{2,1,0:T(8,128)(2,1)} %bitcast.4), custom_call_target="tpu_custom_call" | custom-call | flops 6576668672 | bytes 7340032 | tf_op jit(solution)/shard_map/pallas_call | solution.py:354
  70.3 1.6 %copy.11 = f32[256,128]{1,0:T(8,128)} copy(f32[256,128]{1,0:T(8,128)} %get-tuple-element.8) | data formatting | bytes 262144
  71.9 1.2 %copy.12 = f32[256]{0:T(256)} copy(f32[256]{0:T(256)} %bitcast.5) | data formatting | bytes 2048

commit v4 on v3

--- a/solution.py
+++ b/solution.py
@@ -11,7 +11,7 @@
 MESH = pl.DeviceIdType.MESH
 COMP = 4
 
-STEPS = ((0, 0), (1, 0), (1, 1), (1, 2), (1, 3), (0, 1), (0, 2), (0, 3))
+STEPS = ((1, 0), (1, 1), (1, 2), (1, 3), (0, 0), (0, 1), (0, 2), (0, 3))
 LAST_PARTS = 4
 
 
@@ -143,7 +143,7 @@
             for k in which:
                 y_copy(k).start()
 
-    y_start(0, 1)
+    y_start(0, 1, 2)
 
     first = jnp.where(u >= 1, 1, 0)
 
@@ -281,11 +281,9 @@
             gram_own[low + i] = part if j == 0 else gram_own[low + i] + part
 
     column(0, 0)
-    y_start(2)
+    y_start(3)
     for t in range(count):
         column(t + 1, 0)
-        if t == 0:
-            y_start(3)
         compute(t - 2, 0)
         column(t, 1)
         compute(t - 2, 1)

time: 73.8 us -> 75.1 us (1.018)
  Pallas kernels: 67.8 us -> 69.6 us
    pallas_call x1, Pallas kernels: 67.8 us -> 69.6 us  [fused(): pl.pallas_call(kernel, out_shape=(jax.ShapeDtypeStruct((spectra, zlocal),...]
where the time goes in v4:
time: 75.1 us; the launch traced here: 74.9 us
  Pallas kernels  69.6 us (93%)
  local copies, waits for them, and re-layouts  4.64 us (6%)
    pallas_call x1, Pallas kernels, fused(): pl.pallas_call(kernel, out_shape=(jax.ShapeDtypeStruct((spectra, zlocal),...  69.6 us
    unnamed x3, local copies, waits for them, and re-layouts  4.64 us

profile of v4, /device:TPU:0, one launch (start us, length us, event | category | flops | bytes accessed | tf_op | source)
XLA Modules:
  0.0 74.9 jit_solution(9309522846467810464)
XLA Ops:
  0.6 1.8 %copy.8 = bf16[448,4,128]{2,0,1:T(8,128)(2,1)} copy(bf16[448,4,128]{2,1,0:T(4,128)(2,1)} %param.7) | data formatting | bytes 917504 | tf_op args[3]
  2.5 69.6 %shard_map.59 = (f32[256,128]{1,0:T(8,128)}, f32[1,256]{1,0:T(1,128)}) custom-call(bf16[256,3584]{1,0:T(8,128)(2,1)} %flux.1, bf16[256,3584]{1,0:T(8,128)(2,1)} %ivar.1, s32[256,3584]{1,0:T(8,128)} %mask.1, bf16[4,448,128]{2,1,0:T(8,128)(2,1)} %bitcast.4), custom_call_target="tpu_custom_call" | custom-call | flops 6576668672 | bytes 7340032 | tf_op jit(solution)/shard_map/pallas_call | solution.py:352
  72.1 1.6 %copy.11 = f32[256,128]{1,0:T(8,128)} copy(f32[256,128]{1,0:T(8,128)} %get-tuple-element.8) | data formatting | bytes 262144
  73.7 1.2 %copy.12 = f32[256]{0:T(256)} copy(f32[256]{0:T(256)} %bitcast.5) | data formatting | bytes 2048
